TPU v7x, 512 devices: a whole 4x8x8 slice. The times are simulated.
512 devices in a mesh: ka: 8 (over z_lo, core), pair: 64 (over y, z_hi, x).
Axes of the slice: x: 4, y: 8, z: 8 (z_hi: 2, z_lo: 4; z = z_hi * 4 + z_lo), core: 2. Of those that a mesh axis runs over, the one named last changes fastest.
Arguments:
- cond_orbitals: bfloat16 [8, 2048, 8192], P('ka', 'pair'), may hold values from -6 to 6
- cond_energy: float32 [8, 8192], P('ka', 'pair'), may hold values from 0.5 to 8
- val_orbitals: bfloat16 [512, 2048], P(('ka', 'pair')), may hold values from -6 to 6
- val_energy: bfloat16 [512], P(('ka', 'pair')), may hold values from -8 to -0.5
- val_slots: int32 [8, 64, 16], P('ka', 'pair'), may hold values from 0 to 511
- owner_count: int32 [8, 64], P('ka', 'pair'), may hold values from 1 to 16, as said below
Outputs:
- response: float32 [8, 2048, 512], P('ka', 'pair')
Inputs may be any that keep to these rules, and one draw needn't show every extreme that they name: `owner_count`: in every lane some owner has exactly 16 live slots.
All inputs are finite; a program needn't handle non-finite values.
Results may differ from a plain program's by a relative error of at most 0.0047.
The roundings to bfloat16 on the way count: a program that leaves them out, or rounds other values in their place, can miss the bound.
Values may be sent and summed in bfloat16 or wider, within the bound.
No kernel may reach another device: no remote copies, remote signals or barrier semaphores. Data moves between devices by JAX's collectives and lax.ppermute only.
A program may use at most 64 MiB of HBM per device.

v0:
```python
import jax
import jax.numpy as jnp
from jax import lax
from jax.sharding import PartitionSpec as P

BC = 128
GA = 16
GB = 128
WIN = 512
SLOTS = 16


def cosine_table(length):
    freq = lax.iota(jnp.float32, length)[:, None]
    point = lax.iota(jnp.float32, length)[None, :]
    factor = jnp.where(freq == 0, jnp.sqrt(1.0 / length), jnp.sqrt(2.0 / length))
    return (factor * jnp.cos(jnp.pi * (point + 0.5) * freq / length)).astype(jnp.bfloat16)


def owner_terms(picked, e_pick, live, cond_block, e_cond, table_a, table_b):
    slots = picked.shape[0]
    pair_real = (
        picked[:, None, :].astype(jnp.float32) * cond_block[None].astype(jnp.float32)
    ).astype(jnp.bfloat16)
    count = slots * cond_block.shape[0]
    rows = pair_real.reshape(count * GA, GB)
    first = jnp.dot(rows, table_b.T, preferred_element_type=jnp.float32).astype(jnp.bfloat16)
    first = first.reshape(count, GA, GB)
    moved = jnp.einsum("ja,pak->pjk", table_a, first, preferred_element_type=jnp.float32)
    moved = moved.astype(jnp.bfloat16).reshape(count, GA * GB)
    weight = live[:, None] * 2.0 / (e_cond[None, :] - e_pick[:, None])
    weighted = (moved[:, :WIN].astype(jnp.float32) * weight.reshape(count, 1)).astype(jnp.bfloat16)
    return (moved, weighted)


def shards(cond_orbitals, cond_energy, val_orbitals, val_energy, val_slots, owner_count):
    cond_block = lax.all_to_all(cond_orbitals, "pair", split_axis=2, concat_axis=1, tiled=True)[0].T
    all_orb, all_energy = (
        lax.all_gather(val_orbitals, ("ka", "pair"), axis=0, tiled=True),
        lax.all_gather(val_energy, ("ka", "pair"), axis=0, tiled=True),
    )
    slots = val_slots[0, 0]
    picked = jnp.take(all_orb, slots, axis=0)
    e_pick = jnp.take(all_energy, slots).astype(jnp.float32)
    live = (lax.iota(jnp.int32, slots.shape[0]) < owner_count[0, 0]).astype(jnp.float32)
    moved, weighted = owner_terms(
        picked, e_pick, live, cond_block, cond_energy[0], cosine_table(GA), cosine_table(GB)
    )
    owners = lax.axis_size("pair")
    grid_len = moved.shape[1]
    own_rows = grid_len // owners
    summed = lax.psum(
        lax.dot_general(
            moved, weighted, (((0,), (0,)), ((), ())), preferred_element_type=jnp.float32
        ),
        "pair",
    )
    mine = lax.dynamic_slice_in_dim(summed, lax.axis_index("pair") * own_rows, own_rows, 0)
    scale = 2.0 / (SLOTS * BC * owners)
    return (mine * scale)[None]


def solution(mesh):
    return jax.shard_map(
        shards,
        mesh=mesh,
        in_specs=(
            P("ka", "pair", None),
            P("ka", "pair"),
            P(("ka", "pair"), None),
            P(("ka", "pair")),
            P("ka", "pair", None),
            P("ka", "pair"),
        ),
        out_specs=P("ka", "pair", None),
        check_vma=False,
    )
```

profile of v0, /device:TPU:2, one launch (start us, length us, event | category | flops | bytes accessed | tf_op | source)
XLA Modules:
  0.0 2326.5 jit_solution(4205094719186806137)
XLA Ops:
  6.5 0.0 copy-start.1
  6.5 0.0 copy-start
  6.5 0.0 all-gather.3.cloned.1.call-start
  6.5 0.7 all-gather.3.cloned.1.call-update
  7.3 8.6 copy.18
  15.9 0.5 broadcast.173
  16.4 45.2 %reduce = bf16[8192,32]{1,0:T(8,128)(2,1)S(1)} reduce(bf16[8192,1,32]{2,1,0:T(2,128)(2,1)} %bitcast.45, bf16[]{:T(256)} %broadcast.173), dimensions={1}, to_apply=%bitcast.34.reduce_sub_computation | reduce | bytes 1048578
  61.6 2.8 reshape.162
  64.4 19.1 all-to-all-start
  83.5 0.0 all-reduce.3.cloned.1.call-start
  84.9 0.1 dynamic-update-slice
  85.0 103.8 %all-reduce = bf16[512]{0:T(512)(128)(2,1)S(1)} all-reduce(bf16[512]{0:T(512)(128)(2,1)S(1)} %dynamic-update-slice), channel_id=1, replica_groups=mesh['ka'=8,'pair'=64] {'ka','pair'}, use_global_device_ids=true, to_apply=%add | all-reduce | flops 512 | bytes 2048
  188.8 0.0 copy-done.1
  188.8 0.7 gather_fusion.1
  189.5 0.0 copy-done
  189.5 0.1 divide_bitcast_fusion
  189.6 0.0 all-to-all-done
  189.6 7.2 reshape.163
  196.8 8.0 copy.19
  204.8 0.1 convert_bitcast_fusion
  204.9 0.2 copy.23
  205.1 0.6 copy.20
  205.7 0.3 copy.21
  206.0 1193.1 %all-gather.3.cloned.1.call-done = bf16[512,1,2048]{2,1,0:T(2,128)(2,1)} async-done(((bf16[1,1,2048]{2,1,0:T(2,128)(2,1)}), bf16[512,1,2048]{2,1,0:T(2,128)(2,1)}) %all-gather.3.cloned.1.call-update) | async-done | bytes 2097168 | tf_op jit(solution)/shard_map/all_gather | solution.py:39
  1399.1 3.5 copy.28
  1402.6 0.6 gather_fusion
  1403.2 0.1 select_convert_fusion
  1403.3 5.4 multiply_convert_fusion
  1408.6 13.5 convert_element_type.68
  1422.1 5.9 convolution_convert_fusion
  1428.0 5.6 convolution_convert_fusion.1
  1433.7 10.9 copy.27
  1444.5 10.6 fusion
  1455.1 0.0 all-reduce.3.cloned.1.call-update
  1455.1 863.1 %all-reduce.3.cloned.1.call-done = f32[2048,512]{1,0:T(8,128)} async-done(((f32[2048,512]{1,0:T(8,128)}), f32[2048,512]{1,0:T(8,128)}) %all-reduce.3.cloned.1.call-update) | async-done | bytes 4194320 | tf_op jit(solution)/shard_map/psum | solution.py:52
  2318.2 1.5 multiply_bitcast_fusion
  (7 shorter events, 0.0 us)
Async XLA Ops:
  6.5 182.2 %copy-start.1 = (s32[1,1,16]{2,1,0:T(1,128)S(1)}, s32[1,1,16]{2,1,0:T(1,128)}, u32[]{:S(2)}) copy-start(s32[1,1,16]{2,1,0:T(1,128)} %param.10) | copy-start | bytes 196
  6.5 183.0 %copy-start = (f32[1,128]{1,0:T(1,128)S(1)}, f32[1,128]{1,0:T(1,128)}, u32[]{:S(2)}) copy-start(f32[1,128]{1,0:T(1,128)} %param.7) | copy-start | bytes 1540
  6.5 1392.6 %all-gather.3.cloned.1.call-start = ((), (), s32[]{:S(2)}) async-start(), calls=%async_computation.2 | async-start | bytes 4202496 | tf_op jit(solution)/shard_map/all_gather | solution.py:39
  64.4 125.2 %all-to-all-start = ((bf16[64,2,2048]{2,1,0:T(2,128)(2,1)}), bf16[64,2,2048]{2,1,0:T(2,128)(2,1)S(1)}, u32[]{:S(2)}, u32[]{:S(2)}) async-start(bf16[64,2,2048]{2,1,0:T(2,128)(2,1)} %reshape.162), calls=%async_computation | async-start | bytes 1048576 | tf_op jit(solution)/shard_map/all_to_all | solution.py:37
  83.5 2234.7 %all-reduce.3.cloned.1.call-start = ((), (), s32[]{:S(2)}) async-start(), calls=%async_computation.1 | async-start | bytes 8388608 | tf_op jit(solution)/shard_map/psum | solution.py:52
Sparse Core Ops, SparseCore 0:
  9.6 1389.4 all-gather.2
  1455.2 862.9 all-reduce.2
where the time goes:
time: 2330 us
  waiting for transfers between devices  2060 us (88%)
  blocking collectives  104 us (4%)
  local copies, waits for them, and re-layouts  57.4 us (2%)
  other arithmetic  52.3 us (2%)
    all_gather x1, waiting for transfers between devices, shards(): lax.all_gather(val_orbitals, ('ka', 'pair'), axis=0, tiled=True)  1190 us
    psum x1, waiting for transfers between devices, shards(): lax.psum(lax.dot_general(moved, weighted, (((0,), (0,)), ((), ())), prefe...  863 us
    unnamed x1, blocking collectives  104 us
  transfers between devices with their start and end apart: 3, of which 2 were waited for; matrix products, arithmetic and copies ran while one was open for 3% of the time, Pallas kernels for 0%

commit v1 on v0

--- a/solution.py
+++ b/solution.py
@@ -36,7 +36,12 @@
 def shards(cond_orbitals, cond_energy, val_orbitals, val_energy, val_slots, owner_count):
     cond_block = lax.all_to_all(cond_orbitals, "pair", split_axis=2, concat_axis=1, tiled=True)[0].T
     all_orb, all_energy = (
-        lax.all_gather(val_orbitals, ("ka", "pair"), axis=0, tiled=True),
+        jnp.concatenate(
+            lax.all_to_all(
+                jnp.stack([val_orbitals] * lax.axis_size(("ka", "pair"))), ("ka", "pair"), 0, 0
+            ),
+            axis=0,
+        ),
         lax.all_gather(val_energy, ("ka", "pair"), axis=0, tiled=True),
     )
     slots = val_slots[0, 0]

time: 2330 us -> 1200 us (0.52)
  waiting for transfers between devices: 2060 us -> 854 us
  blocking collectives: 104 us -> 136 us
    all_gather x1 -> x0, waiting for transfers between devices: 1190 us -> none  [shards(): lax.all_gather(val_orbitals, ('ka', 'pair'), axis=0, tiled=True)]
    unnamed x1, blocking collectives: 104 us -> 136 us
  transfers between devices with their start and end apart: 3 -> 3, of which waited for: 2 -> 1; matrix products, arithmetic and copies ran while one was open for 3% -> 3% of each run, Pallas kernels for 0% -> 0%
where the time goes in v1:
time: 1200 us
  waiting for transfers between devices  854 us (71%)
  blocking collectives  136 us (11%)
  local copies, waits for them, and re-layouts  73 us (6%)
  other arithmetic  65.5 us (5%)
  starting transfers between devices  36.3 us (3%)
  matrix products  22.1 us (2%)
  between operations  14.8 us (1%)
    psum x1, waiting for transfers between devices, shards(): lax.psum(lax.dot_general(moved, weighted, (((0,), (0,)), ((), ())), prefe...  854 us
    unnamed x1, blocking collectives  136 us
    unnamed x3, other arithmetic  45.3 us
    unnamed x17, local copies, waits for them, and re-layouts  43 us
  transfers between devices with their start and end apart: 3, of which 1 were waited for; matrix products, arithmetic and copies ran while one was open for 3% of the time, Pallas kernels for 0%

profile of v1, /device:TPU:2, one launch (start us, length us, event | category | flops | bytes accessed | tf_op | source)
XLA Modules:
  0.0 1201.9 jit_solution(8501460629408461598)
XLA Ops:
  6.5 0.0 copy-start
  6.5 8.6 copy.18
  15.1 0.5 broadcast.177
  15.7 45.2 %reduce.1 = bf16[8192,32]{1,0:T(8,128)(2,1)S(1)} reduce(bf16[8192,1,32]{2,1,0:T(2,128)(2,1)} %bitcast.44, bf16[]{:T(256)} %broadcast.177), dimensions={1}, to_apply=%bitcast.33.reduce_sub_computation | reduce | bytes 1048578
  60.9 2.8 reshape.168
  63.6 19.1 %all-to-all-start.1 = ((bf16[64,2,2048]{2,1,0:T(2,128)(2,1)}), bf16[64,2,2048]{2,1,0:T(2,128)(2,1)S(1)}, u32[]{:S(2)}, u32[]{:S(2)}) async-start(bf16[64,2,2048]{2,1,0:T(2,128)(2,1)} %reshape.168), calls=%async_computation.1 | async-start | bytes 1048576 | tf_op jit(solution)/shard_map/all_to_all | solution.py:37
  82.7 0.0 copy-done
  82.8 4.1 stack.2
  86.9 0.0 copy-start.2
  86.9 0.0 copy-start.1
  86.9 13.2 %reduce.2 = bf16[512,2048]{1,0:T(8,128)(2,1)S(1)} reduce(bf16[512,1,2048]{2,1,0:T(2,128)(2,1)} %stack.2, bf16[]{:T(256)} %broadcast.177), dimensions={1}, to_apply=%stack.2.reduce_sub_computation | reduce | bytes 4194306 | tf_op jit(solution)/shard_map/stack | solution.py:41
  100.1 2.8 reshape.170
  102.9 0.0 all-to-all-done.1
  102.9 17.2 %all-to-all-start = ((bf16[512,2,1024]{2,1,0:T(2,128)(2,1)}), bf16[512,2,1024]{2,1,0:T(2,128)(2,1)S(1)}, u32[]{:S(2)}, u32[]{:S(2)}) async-start(bf16[512,2,1024]{2,1,0:T(2,128)(2,1)} %reshape.170), calls=%async_computation | async-start | bytes 4194304 | tf_op jit(solution)/shard_map/all_to_all | solution.py:40
  120.1 0.0 all-reduce.3.cloned.1.call-start
  121.4 0.1 dynamic-update-slice
  121.6 136.1 %all-reduce = bf16[512]{0:T(512)(128)(2,1)S(1)} all-reduce(bf16[512]{0:T(512)(128)(2,1)S(1)} %dynamic-update-slice), channel_id=1, replica_groups=mesh['ka'=8,'pair'=64] {'ka','pair'}, use_global_device_ids=true, to_apply=%add | all-reduce | flops 512 | bytes 2048
  257.6 0.0 copy-done.2
  257.7 0.7 gather_fusion.1
  258.4 0.0 copy-done.1
  258.4 0.1 divide_bitcast_fusion
  258.5 7.1 reshape.169
  265.6 8.0 copy.19
  273.6 0.1 convert_bitcast_fusion
  273.6 0.2 copy.23
  273.8 1.6 copy.20
  275.4 1.6 copy.21
  277.0 0.0 all-to-all-done
  277.0 6.6 reshape.171
  283.6 3.5 copy.28
  287.1 0.6 gather_fusion
  287.7 0.1 select_convert_fusion
  287.8 5.4 multiply_convert_fusion
  293.1 13.5 %convert_element_type.68 = bf16[32768,128]{1,0:T(8,128)(2,1)} reshape(bf16[16,128,2048]{2,1,0:T(8,128)(2,1)} %multiply_convert_fusion) | data formatting | bytes 16777216 | tf_op jit(solution)/shard_map/convert_element_type | solution.py:24
  306.6 5.9 convolution_convert_fusion
  312.5 5.6 convolution_convert_fusion.1
  318.1 10.9 copy.27
  329.0 10.6 fusion
  339.6 0.0 all-reduce.3.cloned.1.call-update
  339.6 854.0 %all-reduce.3.cloned.1.call-done = f32[2048,512]{1,0:T(8,128)} async-done(((f32[2048,512]{1,0:T(8,128)}), f32[2048,512]{1,0:T(8,128)}) %all-reduce.3.cloned.1.call-update) | async-done | bytes 4194320 | tf_op jit(solution)/shard_map/psum | solution.py:57
  1193.6 1.5 multiply_bitcast_fusion
  (8 shorter events, 0.1 us)
Async XLA Ops:
  6.5 76.2 %copy-start = (bf16[1,2048]{1,0:T(2,128)(2,1)S(1)}, bf16[1,2048]{1,0:T(2,128)(2,1)}, u32[]{:S(2)}) copy-start(bf16[1,2048]{1,0:T(2,128)(2,1)} %param.8) | copy-start | bytes 12292
  63.6 39.3 %all-to-all-start.1 = ((bf16[64,2,2048]{2,1,0:T(2,128)(2,1)}), bf16[64,2,2048]{2,1,0:T(2,128)(2,1)S(1)}, u32[]{:S(2)}, u32[]{:S(2)}) async-start(bf16[64,2,2048]{2,1,0:T(2,128)(2,1)} %reshape.168), calls=%async_computation.1 | async-start | bytes 1048576 | tf_op jit(solution)/shard_map/all_to_all | solution.py:37
  86.9 170.8 %copy-start.2 = (s32[1,1,16]{2,1,0:T(1,128)S(1)}, s32[1,1,16]{2,1,0:T(1,128)}, u32[]{:S(2)}) copy-start(s32[1,1,16]{2,1,0:T(1,128)} %param.10) | copy-start | bytes 196
  86.9 171.5 %copy-start.1 = (f32[1,128]{1,0:T(1,128)S(1)}, f32[1,128]{1,0:T(1,128)}, u32[]{:S(2)}) copy-start(f32[1,128]{1,0:T(1,128)} %param.7) | copy-start | bytes 1540
  102.9 174.1 %all-to-all-start = ((bf16[512,2,1024]{2,1,0:T(2,128)(2,1)}), bf16[512,2,1024]{2,1,0:T(2,128)(2,1)S(1)}, u32[]{:S(2)}, u32[]{:S(2)}) async-start(bf16[512,2,1024]{2,1,0:T(2,128)(2,1)} %reshape.170), calls=%async_computation | async-start | bytes 4194304 | tf_op jit(solution)/shard_map/all_to_all | solution.py:40
  120.1 1073.5 %all-reduce.3.cloned.1.call-start = ((), (), s32[]{:S(2)}) async-start(), calls=%async_computation.2 | async-start | bytes 8388608 | tf_op jit(solution)/shard_map/psum | solution.py:57
Sparse Core Ops, SparseCore 0:
  339.8 853.8 all-reduce.2
